TPU v7x, 512 devices: a whole 4x8x8 slice. The times are simulated.
512 devices in a mesh: dp: 32 (over x, y_lo, core), vocab: 16 (over z, y_hi).
Axes of the slice: x: 4, y: 8 (y_hi: 2, y_lo: 4; y = y_hi * 4 + y_lo), z: 8, core: 2. Of those that a mesh axis runs over, the one named last changes fastest.
Arguments:
- hidden: bfloat16 [7168, 4096], P('dp'), may hold values from -6 to 6
- head_weight: bfloat16 [4096, 16384], P('dp', 'vocab'), may hold values from -0.09375 to 0.09375
- head_bias: float32 [16384], P('vocab'), may hold values from -1 to 1
- lengths: int32 [64, 2], P('dp'), may hold values from 1 to 80, as said below
- positives: int32 [64], P('dp'), may hold values from 0 to 63, each once
Outputs:
- hidden_grad: bfloat16 [7168, 4096], P(('dp', 'vocab'))
Inputs may be any that keep to these rules, and one draw needn't show every extreme that they name: `lengths`: query counts are at most 32, passage counts at most 80; the first slots of each are used.
All inputs are finite; a program needn't handle non-finite values.
Results may differ from a plain program's by a relative error of at most 0.0064.
Values may be sent and summed in bfloat16 or wider, within the bound.
A program may use at most 64 MiB of HBM per device.

v0:
```python
import jax
import jax.numpy as jnp
from jax import lax
from jax.sharding import PartitionSpec as P

QLEN = 32
POOL_TEMP = 0.25
SCORE_TEMP = 0.01
LOSS_SCALE = 65536.0


def row_mask(lengths, rows_pair):
    position = lax.broadcasted_iota(jnp.int32, (1, rows_pair), 1)
    is_query = position < QLEN
    offset = jnp.where(is_query, position, position - QLEN)
    limit_len = jnp.where(is_query, lengths[:, 0:1], lengths[:, 1:2])
    return (offset < limit_len).astype(jnp.float32)


def pool_terms(logits, token_mask):
    softened = jax.nn.softplus(logits)
    boosted = token_mask[:, :, None] * jnp.exp(jnp.log1p(softened) / POOL_TEMP)
    return (softened, boosted)


def pooled_vectors(boosted, lengths):
    query_sum = jnp.sum(boosted[:, :QLEN], axis=1)
    passage_sum = jnp.sum(boosted[:, QLEN:], axis=1)
    query_vec = POOL_TEMP * jnp.log(query_sum / lengths[:, 0:1].astype(jnp.float32))
    passage_vec = POOL_TEMP * jnp.log(passage_sum / lengths[:, 1:2].astype(jnp.float32))
    return (query_vec, passage_vec, query_sum, passage_sum)


def score_grads(scores, positives, pair_count):
    row_max = jnp.max(scores, axis=1, keepdims=True)
    shifted = jnp.exp(scores - row_max)
    softmax_out = shifted / jnp.sum(shifted, axis=1, keepdims=True)
    target = (positives[:, None] == lax.broadcasted_iota(jnp.int32, (1, pair_count), 1)).astype(
        jnp.float32
    )
    return LOSS_SCALE * (softmax_out - target)


def logit_grads(logits, softened, boosted, query_sum, passage_sum, query_grad, passage_grad):
    pairs_here = logits.shape[0]
    rest_rows = logits.shape[1] - QLEN
    entries = logits.shape[2]
    query_side = jnp.broadcast_to((query_grad / query_sum)[:, None, :], (pairs_here, QLEN, entries))
    passage_side = jnp.broadcast_to(
        (passage_grad / passage_sum)[:, None, :], (pairs_here, rest_rows, entries)
    )
    per_token = jnp.concatenate([query_side, passage_side], axis=1)
    slope = jax.nn.sigmoid(logits) / (1.0 + softened)
    return (boosted * slope * per_token).astype(jnp.bfloat16)


def per_device(hidden, head_weight, head_bias, lengths, positives):
    pairs_dev = lengths.shape[0]
    rows_pair = hidden.shape[0] // pairs_dev
    slice_width = head_bias.shape[0]
    vocab_devices = lax.axis_size("vocab")
    pairs_all = pairs_dev * lax.axis_size("dp")
    score_scale = 1.0 / (SCORE_TEMP * (slice_width * vocab_devices))
    weights = lax.all_gather(head_weight, "dp", axis=0, tiled=True)
    flat_logits = jnp.dot(hidden, weights, preferred_element_type=jnp.float32) + head_bias
    logits = flat_logits.reshape(pairs_dev, rows_pair, slice_width)
    token_mask = row_mask(lengths, rows_pair)
    softened, boosted = pool_terms(logits, token_mask)
    query_vec, passage_vec, query_sum, passage_sum = pooled_vectors(boosted, lengths)
    query_vec = query_vec.astype(jnp.bfloat16)
    passage_vec = passage_vec.astype(jnp.bfloat16)
    passages = lax.all_gather(passage_vec, "dp", axis=0, tiled=True)
    partial_value = lax.dot_general(
        query_vec, passages, (((1,), (1,)), ((), ())), preferred_element_type=jnp.float32
    )
    scores = score_scale * lax.psum(partial_value, "vocab")
    score_grad = score_grads(scores, positives, pairs_all)
    query_grad = score_scale * jnp.dot(
        score_grad, passages.astype(jnp.float32), precision=lax.Precision.HIGHEST
    )
    query_wide = query_vec.astype(jnp.float32)
    picked = score_grad
    passage_grad = score_scale * lax.psum_scatter(
        lax.dot_general(
            picked, query_wide, (((0,), (0,)), ((), ())), precision=lax.Precision.HIGHEST
        ),
        "dp",
        scatter_dimension=0,
        tiled=True,
    )
    logit_grad = logit_grads(
        logits, softened, boosted, query_sum, passage_sum, query_grad, passage_grad
    )
    logit_grad = logit_grad.reshape(pairs_dev * rows_pair, slice_width)
    picked = logit_grad
    summed = lax.psum_scatter(
        lax.dot_general(
            picked, weights, (((1,), (1,)), ((), ())), preferred_element_type=jnp.float32
        ),
        "vocab",
        scatter_dimension=0,
        tiled=True,
    )
    return summed.astype(jnp.bfloat16)


def solution(mesh):
    return jax.shard_map(
        per_device,
        mesh=mesh,
        in_specs=(P("dp", None), P("dp", "vocab"), P("vocab"), P("dp", None), P("dp")),
        out_specs=P(("dp", "vocab"), None),
        check_vma=False,
    )
```

profile of v0, /device:TPU:94, one launch (start us, length us, event | category | flops | bytes accessed | tf_op | source)
XLA Modules:
  0.0 667.0 jit_solution(6639236065506254835)
XLA Ops:
  6.5 0.7 all-gather.3.cloned.1.call-update
  7.3 0.1 broadcast_in_dim.54
  7.4 0.1 lt.38
  7.5 1.0 slice_reduce_fusion.3
  8.5 0.1 broadcast_in_dim.56
  8.6 0.1 broadcast_in_dim.57
  8.7 0.1 broadcast_in_dim.60
  8.8 1.0 convert_reduce_fusion.1
  9.8 0.1 compare_convert_fusion.1
  9.9 72.9 %all-gather.3.cloned.1.call-done = bf16[4096,1024]{1,0:T(8,128)(2,1)} async-done(((bf16[128,1024]{1,0:T(8,128)(2,1)}), bf16[4096,1024]{1,0:T(8,128)(2,1)}) %all-gather.3.cloned.1.call-update) | async-done | bytes 8388624 | tf_op jit(solution)/shard_map/all_gather | solution.py:64
  82.7 5.4 convolution_add_fusion
  88.2 0.9 fusion.5
  89.1 0.1 fusion.8
  89.2 37.5 %all-gather = bf16[32,2,1024]{2,1,0:T(2,128)(2,1)S(1)} all-gather(bf16[1,2,1024]{2,1,0:T(2,128)(2,1)S(1)} %fusion.8), channel_id=1, replica_groups=mesh['dp'=32,'vocab'=16] {'dp'}, dimensions={0}, use_global_device_ids=true | all-gather | bytes 135168 | tf_op jit(solution)/shard_map/all_gather | solution.py:72
  126.8 0.2 fusion.14
  127.0 51.4 %psum.7 = f32[2,64]{1,0:T(2,128)S(1)} all-reduce(f32[2,64]{1,0:T(2,128)S(1)} %fusion.14), channel_id=1, replica_groups=mesh['dp'=32,'vocab'=16] {'vocab'}, use_global_device_ids=true, to_apply=%region_2.3 | all-reduce | flops 128 | bytes 1024 | tf_op jit(solution)/shard_map/psum | solution.py:76
  178.4 0.1 multiply_reduce_fusion
  178.5 0.2 fusion.10
  178.7 1.1 fusion.11
  179.8 1.3 dynamic-slice
  181.8 0.2 fusion.1
  182.0 272.1 %all-reduce.5.cloned.1.call-done = f32[64,1024]{1,0:T(8,128)} async-done(((f32[64,1024]{1,0:T(8,128)}), f32[64,1024]{1,0:T(8,128)}) %all-reduce.5.cloned.1.call-update) | async-done | bytes 262160
  454.2 0.8 fusion.7
  455.1 1.1 fusion.6
  456.2 7.9 %fusion.15 = f32[224,4096]{1,0:T(8,128)} fusion(bf16[224,1024]{1,0:T(8,128)(2,1)S(1)} %fusion.6, bf16[4096,1024]{1,0:T(8,128)(2,1)} %all-gather.3.cloned.1.call-done), kind=kOutput, calls=%fused_computation.38 | convolution fusion | flops 1879048192 | bytes 12517376 | tf_op jit(solution)/shard_map/dot_general | solution.py:97
  464.1 181.7 %fusion = f32[16,4096]{1,0:T(8,128)S(1)} fusion(f32[224,4096]{1,0:T(8,128)} %fusion.15), kind=kCustom, calls=%all-reduce-scatter | all-reduce-scatter fusion | flops 1048577 | bytes 3934208
  645.8 3.3 collective-permute-start
  649.2 3.5 collective-permute-start.1
  652.7 1.3 dynamic-slice.6
  654.6 4.2 collective-permute-done.1
  658.8 0.6 concatenate.7
  659.4 0.7 dynamic-slice_convert_fusion
  (22 shorter events, 0.5 us)
Async XLA Ops:
  6.5 76.2 %copy-start = (bf16[224,4096]{1,0:T(8,128)(2,1)S(1)}, bf16[224,4096]{1,0:T(8,128)(2,1)}, u32[]{:S(2)}) copy-start(bf16[224,4096]{1,0:T(8,128)(2,1)} %param.5) | copy-start | bytes 5505028
  6.5 76.2 %all-gather.3.cloned.1.call-start = ((), (), s32[]{:S(2)}) async-start(), calls=%async_computation | async-start | bytes 8650752 | tf_op jit(solution)/shard_map/all_gather | solution.py:64
  7.3 446.9 %all-reduce.5.cloned.1.call-start = ((), (), s32[]{:S(2)}) async-start(), calls=%async_computation.1 | async-start | bytes 524288
  9.9 168.8 %copy-start.1 = (s32[2]{0:T(128)S(1)}, s32[2]{0:T(128)}, u32[]{:S(2)}) copy-start(s32[2]{0:T(128)} %param.9) | copy-start | bytes 28
  645.8 13.0 %collective-permute-start = (bf16[16,4096]{1,0:T(8,128)(2,1)S(1)}, bf16[16,4096]{1,0:T(8,128)(2,1)S(1)}, u32[]{:S(2)}, u32[]{:S(2)}) collective-permute-start(bf16[16,4096]{1,0:T(8,128)(2,1)S(1)} %convert), channel_id=1, source_target_pairs={{0,1},{1,2},{2,3},{3,4},{4,5},{5,6},{6,7},{7,8},{8,9},{9,10},{10,1... | collective-permute-start | bytes 393224
  649.2 9.7 %collective-permute-start.1 = (bf16[14,4096]{1,0:T(8,128)(2,1)S(1)}, bf16[14,4096]{1,0:T(8,128)(2,1)S(1)}, u32[]{:S(2)}, u32[]{:S(2)}) collective-permute-start(bf16[14,4096]{1,0:T(8,128)(2,1)S(1)} %slice.20), channel_id=1, source_target_pairs={{0,2},{1,3},{2,4},{3,5},{4,6},{5,7},{6,8},{7,9},{8,10},{9,11},{10,... | collective-permute-start | bytes 344072
Sparse Core Ops, SparseCore 0:
  9.5 73.1 all-gather.2
  179.9 274.1 all-reduce.4
where the time goes:
time: 667 us
  waiting for transfers between devices  350 us (52%)
  blocking collectives  271 us (41%)
  matrix products  14.9 us (2%)
  between operations  14.9 us (2%)
  starting transfers between devices  6.84 us (1%)
    unnamed x5, waiting for transfers between devices  277 us
    unnamed x1, blocking collectives  182 us
    all_gather x1, waiting for transfers between devices, per_device(): weights = lax.all_gather(head_weight, 'dp', axis=0, tiled=True)  72.9 us
    psum x1, blocking collectives, per_device(): scores = score_scale * lax.psum(partial_value, 'vocab')  51.4 us
    all_gather x1, blocking collectives, per_device(): passages = lax.all_gather(passage_vec, 'dp', axis=0, tiled=True)  37.5 us
  transfers between devices with their start and end apart: 4, of which 3 were waited for; matrix products, arithmetic and copies ran while one was open for 1% of the time, Pallas kernels for 0%

commit v1 on v0

--- a/solution.py
+++ b/solution.py
@@ -1,3 +1,4 @@
+import functools
 import jax
 import jax.numpy as jnp
 from jax import lax
@@ -7,6 +8,21 @@
 POOL_TEMP = 0.25
 SCORE_TEMP = 0.01
 LOSS_SCALE = 65536.0
+
+
+def _turn_stocks(local, mesh_name):
+    return jnp.concatenate(
+        lax.all_to_all(
+            jnp.stack([local] * lax.psum(1, axis_name=mesh_name), axis=0),
+            concat_axis=0,
+            split_axis=0,
+            axis_name=mesh_name,
+        ),
+        axis=0,
+    )
+
+
+read_terms = functools.partial(_turn_stocks, mesh_name="dp")
 
 
 def row_mask(lengths, rows_pair):
@@ -69,7 +85,7 @@
     query_vec, passage_vec, query_sum, passage_sum = pooled_vectors(boosted, lengths)
     query_vec = query_vec.astype(jnp.bfloat16)
     passage_vec = passage_vec.astype(jnp.bfloat16)
-    passages = lax.all_gather(passage_vec, "dp", axis=0, tiled=True)
+    passages = read_terms(passage_vec)
     partial_value = lax.dot_general(
         query_vec, passages, (((1,), (1,)), ((), ())), preferred_element_type=jnp.float32
     )

time: 667 us -> 643 us (0.964)
  blocking collectives: 271 us -> 233 us
  starting transfers between devices: 6.84 us -> 14.7 us
    all_gather x1 -> x0, blocking collectives: 37.5 us -> none  [per_device(): passages = lax.all_gather(passage_vec, 'dp', axis=0, tiled=True)]
    all_to_all x0 -> x1, starting transfers between devices: none -> 7.82 us  [_turn_stocks(): lax.all_to_all(jnp.stack([local] * lax.psum(1, axis_name=mesh_name), axis...]
  transfers between devices with their start and end apart: 4 -> 5, of which waited for: 3 -> 4; matrix products, arithmetic and copies ran while one was open for 1% -> 1% of each run, Pallas kernels for 0% -> 0%
where the time goes in v1:
time: 643 us; the launch traced here: 642 us
  waiting for transfers between devices  352 us (55%)
  blocking collectives  233 us (36%)
  matrix products  14.9 us (2%)
  between operations  14.9 us (2%)
  starting transfers between devices  14.7 us (2%)
  local copies, waits for them, and re-layouts  7.18 us (1%)
    unnamed x5, waiting for transfers between devices  275 us
    unnamed x1, blocking collectives  182 us
    all_gather x1, waiting for transfers between devices, per_device(): weights = lax.all_gather(head_weight, 'dp', axis=0, tiled=True)  73.4 us
    psum x1, blocking collectives, per_device(): scores = score_scale * lax.psum(partial_value, 'vocab')  51.5 us
  transfers between devices with their start and end apart: 5, of which 4 were waited for; matrix products, arithmetic and copies ran while one was open for 1% of the time, Pallas kernels for 0%

profile of v1, /device:TPU:94, one launch (start us, length us, event | category | flops | bytes accessed | tf_op | source)
XLA Modules:
  0.0 642.1 jit_solution(9431244980472925280)
XLA Ops:
  6.5 0.7 all-gather.2.cloned.1.call-update
  7.3 1.0 convert_reduce_fusion.1
  8.2 1.0 slice_reduce_fusion.3
  9.3 73.4 %all-gather.2.cloned.1.call-done = bf16[4096,1024]{1,0:T(8,128)(2,1)} async-done(((bf16[128,1024]{1,0:T(8,128)(2,1)}), bf16[4096,1024]{1,0:T(8,128)(2,1)}) %all-gather.2.cloned.1.call-update) | async-done | bytes 8388624 | tf_op jit(solution)/shard_map/all_gather | solution.py:80
  82.7 5.4 convolution_add_fusion
  88.2 0.9 fusion.5
  89.1 1.0 copy-done.1
  90.2 0.7 stack.2
  90.9 7.8 %all-to-all-start = ((bf16[32,2,1024]{2,1,0:T(2,128)(2,1)}), bf16[32,2,1024]{2,1,0:T(2,128)(2,1)S(1)}, u32[]{:S(2)}, u32[]{:S(2)}) async-start(bf16[32,2,1024]{2,1,0:T(2,128)(2,1)} %stack.2), calls=%async_computation | async-start | bytes 262144 | tf_op jit(solution)/shard_map/all_to_all | solution.py:15
  98.8 0.1 broadcast_in_dim.54
  98.9 0.1 lt.38
  99.1 0.1 broadcast_in_dim.57
  99.3 1.0 slice_reduce_fusion.1
  100.3 3.1 all-to-all-done
  103.4 0.2 fusion.13
  103.6 51.5 %psum.7 = f32[2,64]{1,0:T(2,128)S(1)} all-reduce(f32[2,64]{1,0:T(2,128)S(1)} %fusion.13), channel_id=1, replica_groups=mesh['dp'=32,'vocab'=16] {'vocab'}, use_global_device_ids=true, to_apply=%region_2.3 | all-reduce | flops 128 | bytes 1024 | tf_op jit(solution)/shard_map/psum | solution.py:92
  155.2 0.1 multiply_reduce_fusion
  155.3 0.2 fusion.9
  155.5 1.1 fusion.10
  156.6 1.3 dynamic-slice
  158.5 0.2 fusion.1
  158.8 270.5 %all-reduce.5.cloned.1.call-done = f32[64,1024]{1,0:T(8,128)} async-done(((f32[64,1024]{1,0:T(8,128)}), f32[64,1024]{1,0:T(8,128)}) %all-reduce.5.cloned.1.call-update) | async-done | bytes 262160
  429.2 0.8 fusion.7
  430.2 1.1 fusion.6
  431.3 7.9 %fusion.14 = f32[224,4096]{1,0:T(8,128)} fusion(bf16[224,1024]{1,0:T(8,128)(2,1)S(1)} %fusion.6, bf16[4096,1024]{1,0:T(8,128)(2,1)} %all-gather.2.cloned.1.call-done), kind=kOutput, calls=%fused_computation.37 | convolution fusion | flops 1879048192 | bytes 12517376 | tf_op jit(solution)/shard_map/dot_general | solution.py:113
  439.2 181.7 %fusion = f32[16,4096]{1,0:T(8,128)S(1)} fusion(f32[224,4096]{1,0:T(8,128)} %fusion.14), kind=kCustom, calls=%all-reduce-scatter | all-reduce-scatter fusion | flops 1048577 | bytes 3934208
  620.9 3.3 collective-permute-start
  624.3 3.5 collective-permute-start.1
  627.8 1.3 dynamic-slice.6
  629.7 4.2 collective-permute-done.1
  633.9 0.6 concatenate.7
  634.5 0.7 dynamic-slice_convert_fusion
  (26 shorter events, 0.8 us)
Async XLA Ops:
  6.5 76.2 %copy-start = (bf16[224,4096]{1,0:T(8,128)(2,1)S(1)}, bf16[224,4096]{1,0:T(8,128)(2,1)}, u32[]{:S(2)}) copy-start(bf16[224,4096]{1,0:T(8,128)(2,1)} %param.5) | copy-start | bytes 5505028
  6.5 76.2 %all-gather.2.cloned.1.call-start = ((), (), s32[]{:S(2)}) async-start(), calls=%async_computation.1 | async-start | bytes 8650752 | tf_op jit(solution)/shard_map/all_gather | solution.py:80
  9.3 146.2 %copy-start.2 = (s32[2]{0:T(128)S(1)}, s32[2]{0:T(128)}, u32[]{:S(2)}) copy-start(s32[2]{0:T(128)} %param.9) | copy-start | bytes 28
  89.1 1.0 copy-start.1
  90.9 12.4 %all-to-all-start = ((bf16[32,2,1024]{2,1,0:T(2,128)(2,1)}), bf16[32,2,1024]{2,1,0:T(2,128)(2,1)S(1)}, u32[]{:S(2)}, u32[]{:S(2)}) async-start(bf16[32,2,1024]{2,1,0:T(2,128)(2,1)} %stack.2), calls=%async_computation | async-start | bytes 262144 | tf_op jit(solution)/shard_map/all_to_all | solution.py:15
  98.7 330.5 %all-reduce.5.cloned.1.call-start = ((), (), s32[]{:S(2)}) async-start(), calls=%async_computation.2 | async-start | bytes 524288
  620.9 13.0 %collective-permute-start = (bf16[16,4096]{1,0:T(8,128)(2,1)S(1)}, bf16[16,4096]{1,0:T(8,128)(2,1)S(1)}, u32[]{:S(2)}, u32[]{:S(2)}) collective-permute-start(bf16[16,4096]{1,0:T(8,128)(2,1)S(1)} %convert), channel_id=1, source_target_pairs={{0,1},{1,2},{2,3},{3,4},{4,5},{5,6},{6,7},{7,8},{8,9},{9,10},{10,1... | collective-permute-start | bytes 393224
  624.3 9.7 %collective-permute-start.1 = (bf16[14,4096]{1,0:T(8,128)(2,1)S(1)}, bf16[14,4096]{1,0:T(8,128)(2,1)S(1)}, u32[]{:S(2)}, u32[]{:S(2)}) collective-permute-start(bf16[14,4096]{1,0:T(8,128)(2,1)S(1)} %slice.20), channel_id=1, source_target_pairs={{0,2},{1,3},{2,4},{3,5},{4,6},{5,7},{6,8},{7,9},{8,10},{9,11},{10,... | collective-permute-start | bytes 344072
Sparse Core Ops, SparseCore 0:
  9.5 73.1 all-gather.1
  156.7 272.4 all-reduce.4

commit v2 on v0

--- a/solution.py
+++ b/solution.py
@@ -2,11 +2,17 @@
 import jax.numpy as jnp
 from jax import lax
 from jax.sharding import PartitionSpec as P
+from jax.lax import all_gather
 
 QLEN = 32
 POOL_TEMP = 0.25
 SCORE_TEMP = 0.01
 LOSS_SCALE = 65536.0
+
+
+def _bind_cards(xx, link_axis):
+    next_value = jnp.sum(all_gather(xx, link_axis), axis=0)
+    return next_value
 
 
 def row_mask(lengths, rows_pair):
@@ -73,7 +79,7 @@
     partial_value = lax.dot_general(
         query_vec, passages, (((1,), (1,)), ((), ())), preferred_element_type=jnp.float32
     )
-    scores = score_scale * lax.psum(partial_value, "vocab")
+    scores = score_scale * _bind_cards(partial_value, "vocab")
     score_grad = score_grads(scores, positives, pairs_all)
     query_grad = score_scale * jnp.dot(
         score_grad, passages.astype(jnp.float32), precision=lax.Precision.HIGHEST

time: 667 us -> 666 us (level)
    psum x1 -> x0, blocking collectives: 51.4 us -> none  [per_device(): scores = score_scale * lax.psum(partial_value, 'vocab')]
    all_gather x0 -> x1, blocking collectives: none -> 50.2 us  [_bind_cards(): next_value = jnp.sum(all_gather(xx, link_axis), axis=0)]
where the time goes in v2:
time: 666 us; the launch traced here: 665 us
  waiting for transfers between devices  350 us (53%)
  blocking collectives  269 us (40%)
  matrix products  14.9 us (2%)
  between operations  14.9 us (2%)
  starting transfers between devices  6.85 us (1%)
    unnamed x5, waiting for transfers between devices  277 us
    unnamed x1, blocking collectives  182 us
    all_gather x1, waiting for transfers between devices, per_device(): weights = lax.all_gather(head_weight, 'dp', axis=0, tiled=True)  72.9 us
    all_gather x1, blocking collectives, _bind_cards(): next_value = jnp.sum(all_gather(xx, link_axis), axis=0)  50.2 us
    all_gather x1, blocking collectives, per_device(): passages = lax.all_gather(passage_vec, 'dp', axis=0, tiled=True)  37.5 us
  transfers between devices with their start and end apart: 4, of which 3 were waited for; matrix products, arithmetic and copies ran while one was open for 1% of the time, Pallas kernels for 0%

profile of v2, /device:TPU:94, one launch (start us, length us, event | category | flops | bytes accessed | tf_op | source)
XLA Modules:
  0.0 665.4 jit_solution(11472269314277729454)
XLA Ops:
  6.5 0.7 all-gather.5.cloned.1.call-update
  7.3 0.1 broadcast_in_dim.54
  7.4 0.1 lt.38
  7.5 1.0 slice_reduce_fusion.3
  8.5 0.1 broadcast_in_dim.56
  8.6 0.1 broadcast_in_dim.57
  8.7 0.1 broadcast_in_dim.60
  8.8 1.0 convert_reduce_fusion.1
  9.8 0.1 compare_convert_fusion.1
  9.9 72.9 %all-gather.5.cloned.1.call-done = bf16[4096,1024]{1,0:T(8,128)(2,1)} async-done(((bf16[128,1024]{1,0:T(8,128)(2,1)}), bf16[4096,1024]{1,0:T(8,128)(2,1)}) %all-gather.5.cloned.1.call-update) | async-done | bytes 8388624 | tf_op jit(solution)/shard_map/all_gather | solution.py:70
  82.7 5.4 convolution_add_fusion
  88.2 0.9 fusion.5
  89.1 0.1 fusion.8
  89.2 37.5 %all-gather.1 = bf16[32,2,1024]{2,1,0:T(2,128)(2,1)S(1)} all-gather(bf16[1,2,1024]{2,1,0:T(2,128)(2,1)S(1)} %fusion.8), channel_id=1, replica_groups=mesh['dp'=32,'vocab'=16] {'dp'}, dimensions={0}, use_global_device_ids=true | all-gather | bytes 135168 | tf_op jit(solution)/shard_map/all_gather | solution.py:78
  126.8 0.2 convolution_bitcast_fusion
  127.0 50.2 %all-gather.2 = f32[16,2,64]{2,1,0:T(2,128)S(1)} all-gather(f32[1,2,64]{2,1,0:T(2,128)S(1)} %convolution_bitcast_fusion), channel_id=2, replica_groups=mesh['dp'=32,'vocab'=16] {'vocab'}, dimensions={0}, use_global_device_ids=true | all-gather | bytes 8704 | tf_op jit(solution)/shard_map/all_gather | solution.py:14
  177.2 0.1 multiply_reduce_fusion
  177.4 0.2 fusion.10
  177.6 1.1 fusion.11
  178.7 1.3 dynamic-slice
  180.6 0.2 fusion.1
  180.9 271.7 %all-reduce.5.cloned.1.call-done = f32[64,1024]{1,0:T(8,128)} async-done(((f32[64,1024]{1,0:T(8,128)}), f32[64,1024]{1,0:T(8,128)}) %all-reduce.5.cloned.1.call-update) | async-done | bytes 262160
  452.6 0.8 fusion.7
  453.5 1.1 fusion.6
  454.7 7.9 %fusion.14 = f32[224,4096]{1,0:T(8,128)} fusion(bf16[224,1024]{1,0:T(8,128)(2,1)S(1)} %fusion.6, bf16[4096,1024]{1,0:T(8,128)(2,1)} %all-gather.5.cloned.1.call-done), kind=kOutput, calls=%fused_computation.38 | convolution fusion | flops 1879048192 | bytes 12517376 | tf_op jit(solution)/shard_map/dot_general | solution.py:103
  462.6 181.7 %fusion = f32[16,4096]{1,0:T(8,128)S(1)} fusion(f32[224,4096]{1,0:T(8,128)} %fusion.14), kind=kCustom, calls=%all-reduce-scatter | all-reduce-scatter fusion | flops 1048577 | bytes 3934208
  644.3 3.3 collective-permute-start
  647.6 3.5 collective-permute-start.1
  651.1 1.3 dynamic-slice.6
  653.1 4.2 collective-permute-done.1
  657.3 0.6 concatenate.7
  657.9 0.7 dynamic-slice_convert_fusion
  (23 shorter events, 0.5 us)
Async XLA Ops:
  6.5 76.2 %copy-start = (bf16[224,4096]{1,0:T(8,128)(2,1)S(1)}, bf16[224,4096]{1,0:T(8,128)(2,1)}, u32[]{:S(2)}) copy-start(bf16[224,4096]{1,0:T(8,128)(2,1)} %param.5) | copy-start | bytes 5505028
  6.5 76.2 %all-gather.5.cloned.1.call-start = ((), (), s32[]{:S(2)}) async-start(), calls=%async_computation | async-start | bytes 8650752 | tf_op jit(solution)/shard_map/all_gather | solution.py:70
  7.3 445.3 %all-reduce.5.cloned.1.call-start = ((), (), s32[]{:S(2)}) async-start(), calls=%async_computation.1 | async-start | bytes 524288
  9.9 167.7 %copy-start.1 = (s32[2]{0:T(128)S(1)}, s32[2]{0:T(128)}, u32[]{:S(2)}) copy-start(s32[2]{0:T(128)} %param.9) | copy-start | bytes 28
  644.3 13.0 %collective-permute-start = (bf16[16,4096]{1,0:T(8,128)(2,1)S(1)}, bf16[16,4096]{1,0:T(8,128)(2,1)S(1)}, u32[]{:S(2)}, u32[]{:S(2)}) collective-permute-start(bf16[16,4096]{1,0:T(8,128)(2,1)S(1)} %convert), channel_id=1, source_target_pairs={{0,1},{1,2},{2,3},{3,4},{4,5},{5,6},{6,7},{7,8},{8,9},{9,10},{10,1... | collective-permute-start | bytes 393224
  647.6 9.7 %collective-permute-start.1 = (bf16[14,4096]{1,0:T(8,128)(2,1)S(1)}, bf16[14,4096]{1,0:T(8,128)(2,1)S(1)}, u32[]{:S(2)}, u32[]{:S(2)}) collective-permute-start(bf16[14,4096]{1,0:T(8,128)(2,1)S(1)} %slice.20), channel_id=1, source_target_pairs={{0,2},{1,3},{2,4},{3,5},{4,6},{5,7},{6,8},{7,9},{8,10},{9,11},{10,... | collective-permute-start | bytes 344072
Sparse Core Ops, SparseCore 0:
  9.5 73.1 all-gather.4
  178.8 273.7 all-reduce.4
